TPU v7x, 32 devices: a whole 2x2x4 slice. The times are simulated.
32 devices in a mesh: cells: 32 (over z, y, x, core).
Axes of the slice: x: 2, y: 2, z: 4, core: 2. Of those that a mesh axis runs over, the one named last changes fastest.
Arguments:
- source_points: bfloat16 [50, 32768], P(None, 'cells'), may hold values from -15 to 15
- target_points: bfloat16 [50, 32768], P(None, 'cells'), may hold values from -15 to 15
- target_features: bfloat16 [32768, 256], P('cells'), may hold values from -6 to 6
- source_mass: float32 [32768], P('cells'), may hold values from -1 to 1
- target_mass: float32 [32768], P('cells'), may hold values from -1 to 1
- pair_list: int32 [3, 384], P(None, 'cells'), may hold values from 0 to 31, as said below
Outputs:
- source_potential: float32 [32768], P('cells')
- target_potential: float32 [32768], P('cells')
- mapped_features: bfloat16 [32768, 256], P('cells')
Inputs may be any that keep to these rules, and one draw needn't show every extreme that they name: `pair_list`: column s is a slot of device s // 12: row 0 names a source block, row 1 a target block, row 2 is 1 where the slot holds a pair and 0 where it is empty; a device's live slots come first, in an order drawn from the seed, and an empty slot names the device's own block twice. Each source block is paired with 7 target blocks within 4 blocks of it around the cycle of 32 blocks: its own, and others drawn from the seed; every pair is listed once. A pair's owner lies in the aligned group of 4 devices that holds its source block; in every group one device owns 12 pairs and the others share the rest as evenly as possible, in an order drawn from the seed.
All inputs are finite; a program needn't handle non-finite values.
Results may differ from a plain program's by a relative error of at most 0.01.
Values may be sent and summed in bfloat16 or wider, within the bound.
A program may use at most 128 MiB of HBM per device.

v0:
```python
import jax
import jax.numpy as jnp
from jax import lax
from jax.sharding import PartitionSpec as P

REACH = 4
GROUP = 4
ITERS = 2


EPSILON = 0.1
LOWEST = -1e30


def shortened(array):

    def short(part):
        return part.astype(jnp.bfloat16) if part.dtype == jnp.float32 else part

    return jax.tree.map(short, array)


def passed_along(value, axis, steps):
    count = lax.axis_size(axis)
    first, last = (max(0, -steps), min(count, count - steps))
    return lax.ppermute(value, axis, [(source, source + steps) for source in range(first, last)])


def passed_along_2(block, axis, distance):
    devices = range(lax.axis_size(axis))
    route = [((i - distance) % len(devices), i) for i in devices]
    return lax.ppermute(block, axis, route)


def merge_pair(first, second):
    higher = jnp.maximum(first[0], second[0])
    summed = first[1] * jnp.exp(first[0] - higher) + second[1] * jnp.exp(second[0] - higher)
    return (higher, summed)


def add_pair(first, second):
    return first + second


def centred(named_blocks, own_index, blocks):
    return (named_blocks - own_index + blocks // 2) % blocks - blocks // 2


def stacked(pieces):
    return jax.tree.map(lambda *entries: jnp.stack(entries), *pieces)


def fetch_source_rows(value, offset):
    return jax.tree.map(
        lambda part, own: part.astype(own.dtype),
        passed_along(shortened(value), "cells", -offset),
        value,
    )


def fetch_target_rows(value, offset):
    return jax.tree.map(
        lambda part, own: part.astype(own.dtype),
        passed_along_2(shortened(value), "cells", -offset),
        value,
    )


def fetch_source_potential(value, offset):
    return passed_along(value, "cells", -offset)


def fetch_target_potential(value, offset):
    return passed_along_2(value, "cells", -offset)


def send_columns(value, offset):
    return passed_along_2(value, "cells", offset)


def send_rows(value, offset):
    return passed_along_2(value, "cells", offset)


def send_mapped(value, offset):
    return passed_along_2(value.astype(jnp.bfloat16), "cells", offset).astype(value.dtype)


def window_of(value, reach, fetch):
    pieces = []
    for offset in range(-reach, reach + 1):
        if offset == 0:
            pieces.append(value)
        else:
            pieces.append(fetch(value, offset))
    return stacked(pieces)


def gather_back(pieces, reach, send, combine, initial):
    result = initial
    for offset in range(-reach, reach + 1):
        piece = jax.tree.map(lambda entry: entry[offset + reach], pieces)
        if offset != 0:
            piece = send(piece, offset)
        result = combine(result, piece)
    return result


def local(source_points, target_points, target_features, source_mass, target_mass, pair_list):
    blocks = lax.axis_size("cells")
    own_index = lax.axis_index("cells")
    coord_dims = source_points.shape[0]
    block_cells = source_points.shape[1]
    feat_width = target_features.shape[1]
    src_reach = GROUP - 1
    tgt_reach = REACH + GROUP - 1
    src_slots = centred(pair_list[0], own_index, blocks) + src_reach
    tgt_slots = centred(pair_list[1], own_index, blocks) + tgt_reach
    count = jnp.sum(pair_list[2])
    src_window, mass_window = window_of((source_points, source_mass), src_reach, fetch_source_rows)
    tgt_window, feat_window = window_of(
        (target_points, target_features), tgt_reach, fetch_target_rows
    )
    src_square = jnp.sum(jnp.square(src_window.astype(jnp.float32)), axis=1)
    tgt_square = jnp.sum(jnp.square(tgt_window.astype(jnp.float32)), axis=1)

    def cost_of(src_pos, tgt_pos):
        inner_products = lax.dot_general(
            src_window[src_pos],
            tgt_window[tgt_pos],
            (((0,), (0,)), ((), ())),
            preferred_element_type=jnp.float32,
        )
        return (
            src_square[src_pos][:, None] + tgt_square[tgt_pos][None, :] - 2.0 * inner_products
        ) / coord_dims

    def initial_pair(window_size):
        return (
            jnp.full((window_size, block_cells), LOWEST, jnp.float32),
            jnp.zeros((window_size, block_cells), jnp.float32),
        )

    source_pot = jnp.zeros((block_cells,), jnp.float32)
    target_pot = jnp.zeros((block_cells,), jnp.float32)
    target_window_pot = None
    for iteration in range(ITERS):
        source_window_pot = window_of(source_pot, src_reach, fetch_source_potential)

        def column_visit(slot_index, carry):
            maxima, totals = carry
            src_pos = src_slots[slot_index]
            tgt_pos = tgt_slots[slot_index]
            scores = (source_window_pot[src_pos][:, None] - cost_of(src_pos, tgt_pos)) / EPSILON
            higher = jnp.max(scores, axis=0)
            summed = jnp.sum(jnp.exp(scores - higher[None, :]), axis=0)
            new_max, new_total = merge_pair((maxima[tgt_pos], totals[tgt_pos]), (higher, summed))
            return (maxima.at[tgt_pos].set(new_max), totals.at[tgt_pos].set(new_total))

        maxima, totals = lax.fori_loop(0, count, column_visit, initial_pair(2 * tgt_reach + 1))
        higher, summed = gather_back(
            (maxima, totals),
            tgt_reach,
            send_columns,
            merge_pair,
            (jnp.full((block_cells,), LOWEST, jnp.float32), jnp.zeros((block_cells,), jnp.float32)),
        )
        target_pot = EPSILON * target_mass - EPSILON * (higher + jnp.log(summed))
        target_window_pot = window_of(target_pot, tgt_reach, fetch_target_potential)

        def row_visit(slot_index, carry):
            maxima, totals = carry
            src_pos = src_slots[slot_index]
            tgt_pos = tgt_slots[slot_index]
            scores = (target_window_pot[tgt_pos][None, :] - cost_of(src_pos, tgt_pos)) / EPSILON
            higher = jnp.max(scores, axis=1)
            summed = jnp.sum(jnp.exp(scores - higher[:, None]), axis=1)
            new_max, new_total = merge_pair((maxima[src_pos], totals[src_pos]), (higher, summed))
            return (maxima.at[src_pos].set(new_max), totals.at[src_pos].set(new_total))

        maxima, totals = lax.fori_loop(0, count, row_visit, initial_pair(2 * src_reach + 1))
        higher, summed = gather_back(
            (maxima, totals),
            src_reach,
            send_rows,
            merge_pair,
            (jnp.full((block_cells,), LOWEST, jnp.float32), jnp.zeros((block_cells,), jnp.float32)),
        )
        source_pot = EPSILON * source_mass - EPSILON * (higher + jnp.log(summed))
    source_window_pot = window_of(source_pot, src_reach, fetch_source_potential)

    def push_visit(slot_index, accumulated):
        src_pos = src_slots[slot_index]
        tgt_pos = tgt_slots[slot_index]
        scores = (
            source_window_pot[src_pos][:, None]
            + target_window_pot[tgt_pos][None, :]
            - cost_of(src_pos, tgt_pos)
        ) / EPSILON - mass_window[src_pos][:, None]
        weight = jnp.exp(scores).astype(jnp.bfloat16)
        contribution = jnp.dot(weight, feat_window[tgt_pos], preferred_element_type=jnp.float32)
        return accumulated.at[src_pos].add(contribution)

    partial_mapped = lax.fori_loop(
        0, count, push_visit, jnp.zeros((2 * src_reach + 1, block_cells, feat_width), jnp.float32)
    )
    mapped = gather_back(
        partial_mapped,
        src_reach,
        send_mapped,
        add_pair,
        jnp.zeros((block_cells, feat_width), jnp.float32),
    )
    return (source_pot, target_pot, mapped.astype(jnp.bfloat16))


def solution(mesh):
    return jax.shard_map(
        local,
        mesh=mesh,
        in_specs=(
            P(None, "cells"),
            P(None, "cells"),
            P("cells", None),
            P("cells"),
            P("cells"),
            P(None, "cells"),
        ),
        out_specs=(P("cells"), P("cells"), P("cells", None)),
        check_vma=False,
    )
```

profile of v0, /device:TPU:1, one launch (start us, length us, event | category | flops | bytes accessed | tf_op | source)
XLA Modules:
  0.0 1179.6 jit_solution(9290332388688042924)
XLA Ops:
  45.5 6.8 collective-permute-done.12
  52.9 6.7 collective-permute-done.13
  59.6 7.5 collective-permute-done.14
  67.1 6.5 collective-permute-done.15
  73.6 8.8 collective-permute-done.16
  82.4 7.4 collective-permute-done.17
  101.4 7.2 collective-permute-done.19
  115.4 51.5 %while.67 = (s32[]{:T(128)}, f32[15,1024]{1,0:T(8,128)S(1)}, f32[15,1024]{1,0:T(8,128)S(1)}, s32[]{:T(128)}, s32[12]{0:T(128)S(1)}, /*index=5*/s32[12]{0:T(128)S...) while((s32[]{:T(128)}, f32[15,1024]{1,0:T(8,128)S(1)}, ...), condition=%wide.region_7.8_spmd, body=%wide.region_3.7_spmd.sunk | while | flops 120592400 | bytes 8720733 | solution.py:160
  169.0 14.2 %collective-permute-start.41 = (f32[1024]{0:T(1024)S(1)}, f32[1024]{0:T(1024)S(1)}, u32[]{:S(2)}, u32[]{:S(2)}) collective-permute-start(f32[1024]{0:T(1024)S(1)} %bitcast.599), channel_id=1, source_target_pairs={{6,0},{7,1},{8,2},{9,3},{10,4},{11,5},{12,6},{13,7},{14,8},{15,9},... | collective-permute-start | bytes 12296 | tf_op jit(solution)/shard_map/ppermute | solution.py:32
  183.2 59.1 %collective-permute-start.52 = (f32[1024]{0:T(1024)S(1)}, f32[1024]{0:T(1024)S(1)}, u32[]{:S(2)}, u32[]{:S(2)}) collective-permute-start(f32[1024]{0:T(1024)S(1)} %bitcast.594), channel_id=1, source_target_pairs={{26,0},{27,1},{28,2},{29,3},{30,4},{31,5},{0,6},{1,7},{2,8},{3,9},... | collective-permute-start | bytes 12296 | tf_op jit(solution)/shard_map/ppermute | solution.py:32
  307.7 52.2 %while.68 = (s32[]{:T(128)}, f32[7,1024]{1,0:T(8,128)S(1)}, f32[7,1024]{1,0:T(8,128)S(1)}, s32[]{:T(128)}, s32[12]{0:T(128)S(1)}, /*index=5*/s32[12]{0:T(128)S(1...) while((s32[]{:T(128)}, f32[7,1024]{1,0:T(8,128)S(1)}, ...), condition=%wide.region_12.13_spmd, body=%wide.region_8.12_spmd.sunk | while | flops 120592400 | bytes 8720733 | solution.py:181
  360.0 11.7 collective-permute-start.73
  371.7 61.9 %collective-permute-start.72 = (f32[1024]{0:T(1024)S(1)}, f32[1024]{0:T(1024)S(1)}, u32[]{:S(2)}, u32[]{:S(2)}) collective-permute-start(f32[1024]{0:T(1024)S(1)} %bitcast.595), channel_id=1, source_target_pairs={{30,0},{31,1},{0,2},{1,3},{2,4},{3,5},{4,6},{5,7},{6,8},{7,9},{8,1... | collective-permute-start | bytes 12296 | tf_op jit(solution)/shard_map/ppermute | solution.py:32
  469.7 51.5 %while.69 = (s32[]{:T(128)}, f32[15,1024]{1,0:T(8,128)S(1)}, f32[15,1024]{1,0:T(8,128)S(1)}, s32[]{:T(128)}, s32[12]{0:T(128)S(1)}, /*index=5*/s32[12]{0:T(128)S...) while((s32[]{:T(128)}, f32[15,1024]{1,0:T(8,128)S(1)}, ...), condition=%wide.region_17.18_spmd, body=%wide.region_13.17_spmd.sunk | while | flops 120592400 | bytes 8720733 | solution.py:160
  525.1 13.1 %collective-permute-start.101 = (f32[1024]{0:T(1024)S(1)}, f32[1024]{0:T(1024)S(1)}, u32[]{:S(2)}, u32[]{:S(2)}) collective-permute-start(f32[1024]{0:T(1024)S(1)} %bitcast.602), channel_id=1, source_target_pairs={{6,0},{7,1},{8,2},{9,3},{10,4},{11,5},{12,6},{13,7},{14,8},{15,9},... | collective-permute-start | bytes 12296 | tf_op jit(solution)/shard_map/ppermute | solution.py:32
  538.2 55.0 %collective-permute-start.112 = (f32[1024]{0:T(1024)S(1)}, f32[1024]{0:T(1024)S(1)}, u32[]{:S(2)}, u32[]{:S(2)}) collective-permute-start(f32[1024]{0:T(1024)S(1)} %bitcast.596), channel_id=1, source_target_pairs={{26,0},{27,1},{28,2},{29,3},{30,4},{31,5},{0,6},{1,7},{2,8},{3,9},... | collective-permute-start | bytes 12296 | tf_op jit(solution)/shard_map/ppermute | solution.py:32
  593.2 6.2 collective-permute-start.111
  662.7 55.7 %while.70 = (s32[]{:T(128)}, f32[7,1024]{1,0:T(8,128)S(1)}, f32[7,1024]{1,0:T(8,128)S(1)}, s32[]{:T(128)}, s32[12]{0:T(128)S(1)}, /*index=5*/s32[12]{0:T(128)S(1...) while((s32[]{:T(128)}, f32[7,1024]{1,0:T(8,128)S(1)}, ...), condition=%wide.region_22.23_spmd, body=%wide.region_18.22_spmd.sunk | while | flops 120592400 | bytes 8720733 | solution.py:181
  718.4 11.6 collective-permute-start.139
  730.0 66.8 %collective-permute-start.138 = (f32[1024]{0:T(1024)S(1)}, f32[1024]{0:T(1024)S(1)}, u32[]{:S(2)}, u32[]{:S(2)}) collective-permute-start(f32[1024]{0:T(1024)S(1)} %bitcast.510), channel_id=1, source_target_pairs={{30,0},{31,1},{0,2},{1,3},{2,4},{3,5},{4,6},{5,7},{6,8},{7,9},{8,1... | collective-permute-start | bytes 12296 | tf_op jit(solution)/shard_map/ppermute | solution.py:32
  806.2 5.8 collective-permute-done.137
  876.6 41.6 %collective-permute-done.155 = bf16[1024,256]{1,0:T(8,128)(2,1)S(1)} collective-permute-done((bf16[1024,256]{1,0:T(8,128)(2,1)S(1)}, bf16[1024,256]{1,0:T(8,128)(2,1)S(1)}, u32[]{:S(2)}, u32[]{:S(2)}) %collective-permute-start.155) | collective-permute-done | bytes 524320 | tf_op jit(solution)/shard_map/ppermute | solution.py:32
  919.1 16.1 %collective-permute-done.156 = bf16[1024,256]{1,0:T(8,128)(2,1)S(1)} collective-permute-done((bf16[1024,256]{1,0:T(8,128)(2,1)S(1)}, bf16[1024,256]{1,0:T(8,128)(2,1)S(1)}, u32[]{:S(2)}, u32[]{:S(2)}) %collective-permute-start.156) | collective-permute-done | bytes 524320 | tf_op jit(solution)/shard_map/ppermute | solution.py:32
  936.8 5.8 collective-permute-start.160
  954.4 6.4 collective-permute-start.164
  966.4 10.5 collective-permute-done.164
  982.2 60.6 %while.71 = (s32[]{:T(128)}, f32[7,1024,256]{2,1,0:T(8,128)}, s32[]{:T(128)}, s32[12]{0:T(128)S(1)}, f32[7,1024]{1,0:T(8,128)S(1)}, /*index=5*/s32[12]{0:T(128)S...) while((s32[]{:T(128)}, f32[7,1024,256]{2,1,0:T(8,128)}, ...), condition=%wide.region_25.26_spmd, body=%wide.region_23.0_spmd.sunk | while | flops 651689984 | bytes 2915172 | solution.py:204
  1046.4 6.3 collective-permute-start.166
  1052.7 11.8 %collective-permute-start.171 = (bf16[1024,256]{1,0:T(8,128)(2,1)S(1)}, bf16[1024,256]{1,0:T(8,128)(2,1)S(1)}, u32[]{:S(2)}, u32[]{:S(2)}) collective-permute-start(bf16[1024,256]{1,0:T(8,128)(2,1)S(1)} %get-tuple-element.567), channel_id=1, source_target_pairs={{29,0},{30,1},{31,2},{0,3},{1,4},{2,5},{3,6},{4,7},{5,8},{6,9},{7,... | collective-permute-start | bytes 1572872 | tf_op jit(solution)/shard_map/ppermute | solution.py:32
  1064.6 72.8 %collective-permute-start.170 = (bf16[1024,256]{1,0:T(8,128)(2,1)S(1)}, bf16[1024,256]{1,0:T(8,128)(2,1)S(1)}, u32[]{:S(2)}, u32[]{:S(2)}) collective-permute-start(bf16[1024,256]{1,0:T(8,128)(2,1)S(1)} %get-tuple-element.568), channel_id=1, source_target_pairs={{30,0},{31,1},{0,2},{1,3},{2,4},{3,5},{4,6},{5,7},{6,8},{7,9},{8,1... | collective-permute-start | bytes 1572872 | tf_op jit(solution)/shard_map/ppermute | solution.py:32
  1143.1 17.1 %collective-permute-done.170 = bf16[1024,256]{1,0:T(8,128)(2,1)S(1)} collective-permute-done((bf16[1024,256]{1,0:T(8,128)(2,1)S(1)}, bf16[1024,256]{1,0:T(8,128)(2,1)S(1)}, u32[]{:S(2)}, u32[]{:S(2)}) %collective-permute-start.170) | collective-permute-done | bytes 524320 | tf_op jit(solution)/shard_map/ppermute | solution.py:32
  1160.2 16.9 %collective-permute-done.169 = bf16[1024,256]{1,0:T(8,128)(2,1)S(1)} collective-permute-done((bf16[1024,256]{1,0:T(8,128)(2,1)S(1)}, bf16[1024,256]{1,0:T(8,128)(2,1)S(1)}, u32[]{:S(2)}, u32[]{:S(2)}) %collective-permute-start.169) | collective-permute-done | bytes 524320 | tf_op jit(solution)/shard_map/ppermute | solution.py:32
  (646 shorter events, 499.6 us)
Async XLA Ops:
  25.6 69.2 %collective-permute-start.9 = (bf16[50,1024]{1,0:T(8,128)(2,1)}, bf16[50,1024]{1,0:T(8,128)(2,1)S(1)}, u32[]{:S(2)}, u32[]{:S(2)}) collective-permute-start(bf16[50,1024]{1,0:T(8,128)(2,1)} %param.34), channel_id=1, source_target_pairs={{1,0},{2,1},{3,2},{4,3},{5,4},{6,5},{7,6},{8,7},{9,8},{10,9},{11,1... | collective-permute-start | bytes 307208 | tf_op jit(solution)/shard_map/ppermute | solution.py:26
  36.1 64.2 %collective-permute-start.11 = (bf16[50,1024]{1,0:T(8,128)(2,1)}, bf16[50,1024]{1,0:T(8,128)(2,1)S(1)}, u32[]{:S(2)}, u32[]{:S(2)}) collective-permute-start(bf16[50,1024]{1,0:T(8,128)(2,1)} %param.34), channel_id=1, source_target_pairs={{3,0},{4,1},{5,2},{6,3},{7,4},{8,5},{9,6},{10,7},{11,8},{12,9},{13... | collective-permute-start | bytes 307208 | tf_op jit(solution)/shard_map/ppermute | solution.py:26
  37.5 59.4 %collective-permute-start.10 = (bf16[50,1024]{1,0:T(8,128)(2,1)}, bf16[50,1024]{1,0:T(8,128)(2,1)S(1)}, u32[]{:S(2)}, u32[]{:S(2)}) collective-permute-start(bf16[50,1024]{1,0:T(8,128)(2,1)} %param.34), channel_id=1, source_target_pairs={{2,0},{3,1},{4,2},{5,3},{6,4},{7,5},{8,6},{9,7},{10,8},{11,9},{12,... | collective-permute-start | bytes 307208 | tf_op jit(solution)/shard_map/ppermute | solution.py:26
  38.8 70.0 %collective-permute-start.23 = (bf16[50,1024]{1,0:T(8,128)(2,1)}, bf16[50,1024]{1,0:T(8,128)(2,1)S(1)}, u32[]{:S(2)}, u32[]{:S(2)}) collective-permute-start(bf16[50,1024]{1,0:T(8,128)(2,1)} %param.35), channel_id=1, source_target_pairs={{5,0},{6,1},{7,2},{8,3},{9,4},{10,5},{11,6},{12,7},{13,8},{14,9},{... | collective-permute-start | bytes 307208 | tf_op jit(solution)/shard_map/ppermute | solution.py:32
  166.9 79.2 %collective-permute-start.53 = (f32[1024]{0:T(1024)S(1)}, f32[1024]{0:T(1024)S(1)}, u32[]{:S(2)}, u32[]{:S(2)}) collective-permute-start(f32[1024]{0:T(1024)S(1)} %bitcast.605), channel_id=1, source_target_pairs={{25,0},{26,1},{27,2},{28,3},{29,4},{30,5},{31,6},{0,7},{1,8},{2,9}... | collective-permute-start | bytes 12296 | tf_op jit(solution)/shard_map/ppermute | solution.py:32
  169.0 77.1 %collective-permute-start.41 = (f32[1024]{0:T(1024)S(1)}, f32[1024]{0:T(1024)S(1)}, u32[]{:S(2)}, u32[]{:S(2)}) collective-permute-start(f32[1024]{0:T(1024)S(1)} %bitcast.599), channel_id=1, source_target_pairs={{6,0},{7,1},{8,2},{9,3},{10,4},{11,5},{12,6},{13,7},{14,8},{15,9},... | collective-permute-start | bytes 12296 | tf_op jit(solution)/shard_map/ppermute | solution.py:32
  183.2 64.8 %collective-permute-start.52 = (f32[1024]{0:T(1024)S(1)}, f32[1024]{0:T(1024)S(1)}, u32[]{:S(2)}, u32[]{:S(2)}) collective-permute-start(f32[1024]{0:T(1024)S(1)} %bitcast.594), channel_id=1, source_target_pairs={{26,0},{27,1},{28,2},{29,3},{30,4},{31,5},{0,6},{1,7},{2,8},{3,9},... | collective-permute-start | bytes 12296 | tf_op jit(solution)/shard_map/ppermute | solution.py:32
  360.0 76.7 %collective-permute-start.73 = (f32[1024]{0:T(1024)S(1)}, f32[1024]{0:T(1024)S(1)}, u32[]{:S(2)}, u32[]{:S(2)}) collective-permute-start(f32[1024]{0:T(1024)S(1)} %bitcast.606), channel_id=1, source_target_pairs={{29,0},{30,1},{31,2},{0,3},{1,4},{2,5},{3,6},{4,7},{5,8},{6,9},{7,... | collective-permute-start | bytes 12296 | tf_op jit(solution)/shard_map/ppermute | solution.py:32
  371.7 70.3 %collective-permute-start.68 = (f32[1024]{0:T(1024)S(1)}, f32[1024]{0:T(1024)S(1)}, u32[]{:S(2)}, u32[]{:S(2)}) collective-permute-start(f32[1024]{0:T(1024)S(1)} %bitcast.601), channel_id=1, source_target_pairs={{3,0},{4,1},{5,2},{6,3},{7,4},{8,5},{9,6},{10,7},{11,8},{12,9},{13... | collective-permute-start | bytes 12296 | tf_op jit(solution)/shard_map/ppermute | solution.py:32
  371.7 71.7 %collective-permute-start.72 = (f32[1024]{0:T(1024)S(1)}, f32[1024]{0:T(1024)S(1)}, u32[]{:S(2)}, u32[]{:S(2)}) collective-permute-start(f32[1024]{0:T(1024)S(1)} %bitcast.595), channel_id=1, source_target_pairs={{30,0},{31,1},{0,2},{1,3},{2,4},{3,5},{4,6},{5,7},{6,8},{7,9},{8,1... | collective-permute-start | bytes 12296 | tf_op jit(solution)/shard_map/ppermute | solution.py:32
  521.2 78.5 %collective-permute-start.113 = (f32[1024]{0:T(1024)S(1)}, f32[1024]{0:T(1024)S(1)}, u32[]{:S(2)}, u32[]{:S(2)}) collective-permute-start(f32[1024]{0:T(1024)S(1)} %bitcast.607), channel_id=1, source_target_pairs={{25,0},{26,1},{27,2},{28,3},{29,4},{30,5},{31,6},{0,7},{1,8},{2,9}... | collective-permute-start | bytes 12296 | tf_op jit(solution)/shard_map/ppermute | solution.py:32
  525.1 75.2 %collective-permute-start.101 = (f32[1024]{0:T(1024)S(1)}, f32[1024]{0:T(1024)S(1)}, u32[]{:S(2)}, u32[]{:S(2)}) collective-permute-start(f32[1024]{0:T(1024)S(1)} %bitcast.602), channel_id=1, source_target_pairs={{6,0},{7,1},{8,2},{9,3},{10,4},{11,5},{12,6},{13,7},{14,8},{15,9},... | collective-permute-start | bytes 12296 | tf_op jit(solution)/shard_map/ppermute | solution.py:32
  538.2 63.3 %collective-permute-start.112 = (f32[1024]{0:T(1024)S(1)}, f32[1024]{0:T(1024)S(1)}, u32[]{:S(2)}, u32[]{:S(2)}) collective-permute-start(f32[1024]{0:T(1024)S(1)} %bitcast.596), channel_id=1, source_target_pairs={{26,0},{27,1},{28,2},{29,3},{30,4},{31,5},{0,6},{1,7},{2,8},{3,9},... | collective-permute-start | bytes 12296 | tf_op jit(solution)/shard_map/ppermute | solution.py:32
  658.3 209.7 %collective-permute-start.152 = (bf16[1024,256]{1,0:T(8,128)(2,1)S(1)}, bf16[1024,256]{1,0:T(8,128)(2,1)}, u32[]{:S(2)}, u32[]{:S(2)}) collective-permute-start(bf16[1024,256]{1,0:T(8,128)(2,1)S(1)} %copy-done), channel_id=1, source_target_pairs={{25,0},{26,1},{27,2},{28,3},{29,4},{30,5},{31,6},{0,7},{1,8},{2,9}... | collective-permute-start | bytes 1572872 | tf_op jit(solution)/shard_map/ppermute | solution.py:32
  718.4 81.9 %collective-permute-start.139 = (f32[1024]{0:T(1024)S(1)}, f32[1024]{0:T(1024)S(1)}, u32[]{:S(2)}, u32[]{:S(2)}) collective-permute-start(f32[1024]{0:T(1024)S(1)} %bitcast.513), channel_id=1, source_target_pairs={{29,0},{30,1},{31,2},{0,3},{1,4},{2,5},{3,6},{4,7},{5,8},{6,9},{7,... | collective-permute-start | bytes 12296 | tf_op jit(solution)/shard_map/ppermute | solution.py:32
  730.0 70.3 %collective-permute-start.134 = (f32[1024]{0:T(1024)S(1)}, f32[1024]{0:T(1024)S(1)}, u32[]{:S(2)}, u32[]{:S(2)}) collective-permute-start(f32[1024]{0:T(1024)S(1)} %bitcast.512), channel_id=1, source_target_pairs={{3,0},{4,1},{5,2},{6,3},{7,4},{8,5},{9,6},{10,7},{11,8},{12,9},{13... | collective-permute-start | bytes 12296 | tf_op jit(solution)/shard_map/ppermute | solution.py:32
  730.0 71.1 %collective-permute-start.138 = (f32[1024]{0:T(1024)S(1)}, f32[1024]{0:T(1024)S(1)}, u32[]{:S(2)}, u32[]{:S(2)}) collective-permute-start(f32[1024]{0:T(1024)S(1)} %bitcast.510), channel_id=1, source_target_pairs={{30,0},{31,1},{0,2},{1,3},{2,4},{3,5},{4,6},{5,7},{6,8},{7,9},{8,1... | collective-permute-start | bytes 12296 | tf_op jit(solution)/shard_map/ppermute | solution.py:32
  796.8 74.2 %collective-permute-start.153 = (bf16[1024,256]{1,0:T(8,128)(2,1)S(1)}, bf16[1024,256]{1,0:T(8,128)(2,1)}, u32[]{:S(2)}, u32[]{:S(2)}) collective-permute-start(bf16[1024,256]{1,0:T(8,128)(2,1)S(1)} %copy-done), channel_id=1, source_target_pairs={{26,0},{27,1},{28,2},{29,3},{30,4},{31,5},{0,6},{1,7},{2,8},{3,9},... | collective-permute-start | bytes 1572872 | tf_op jit(solution)/shard_map/ppermute | solution.py:32
  824.4 50.1 %collective-permute-start.154 = (bf16[1024,256]{1,0:T(8,128)(2,1)S(1)}, bf16[1024,256]{1,0:T(8,128)(2,1)}, u32[]{:S(2)}, u32[]{:S(2)}) collective-permute-start(bf16[1024,256]{1,0:T(8,128)(2,1)S(1)} %copy-done), channel_id=1, source_target_pairs={{27,0},{28,1},{29,2},{30,3},{31,4},{0,5},{1,6},{2,7},{3,8},{4,9},{... | collective-permute-start | bytes 1572872 | tf_op jit(solution)/shard_map/ppermute | solution.py:32
  862.9 101.6 %collective-permute-start.163 = (bf16[1024,256]{1,0:T(8,128)(2,1)S(1)}, bf16[1024,256]{1,0:T(8,128)(2,1)}, u32[]{:S(2)}, u32[]{:S(2)}) collective-permute-start(bf16[1024,256]{1,0:T(8,128)(2,1)S(1)} %copy-done), channel_id=1, source_target_pairs={{5,0},{6,1},{7,2},{8,3},{9,4},{10,5},{11,6},{12,7},{13,8},{14,9},{... | collective-permute-start | bytes 1572872 | tf_op jit(solution)/shard_map/ppermute | solution.py:32
  866.5 96.0 %collective-permute-start.162 = (bf16[1024,256]{1,0:T(8,128)(2,1)S(1)}, bf16[1024,256]{1,0:T(8,128)(2,1)}, u32[]{:S(2)}, u32[]{:S(2)}) collective-permute-start(bf16[1024,256]{1,0:T(8,128)(2,1)S(1)} %copy-done), channel_id=1, source_target_pairs={{4,0},{5,1},{6,2},{7,3},{8,4},{9,5},{10,6},{11,7},{12,8},{13,9},{1... | collective-permute-start | bytes 1572872 | tf_op jit(solution)/shard_map/ppermute | solution.py:32
  867.9 50.3 %collective-permute-start.155 = (bf16[1024,256]{1,0:T(8,128)(2,1)S(1)}, bf16[1024,256]{1,0:T(8,128)(2,1)S(1)}, u32[]{:S(2)}, u32[]{:S(2)}) collective-permute-start(bf16[1024,256]{1,0:T(8,128)(2,1)S(1)} %copy-done), channel_id=1, source_target_pairs={{28,0},{29,1},{30,2},{31,3},{0,4},{1,5},{2,6},{3,7},{4,8},{5,9},{6... | collective-permute-start | bytes 1572872 | tf_op jit(solution)/shard_map/ppermute | solution.py:32
  870.9 64.2 %collective-permute-start.156 = (bf16[1024,256]{1,0:T(8,128)(2,1)S(1)}, bf16[1024,256]{1,0:T(8,128)(2,1)S(1)}, u32[]{:S(2)}, u32[]{:S(2)}) collective-permute-start(bf16[1024,256]{1,0:T(8,128)(2,1)S(1)} %copy-done), channel_id=1, source_target_pairs={{29,0},{30,1},{31,2},{0,3},{1,4},{2,5},{3,6},{4,7},{5,8},{6,9},{7,... | collective-permute-start | bytes 1572872 | tf_op jit(solution)/shard_map/ppermute | solution.py:32
  874.5 61.5 %collective-permute-start.157 = (bf16[1024,256]{1,0:T(8,128)(2,1)S(1)}, bf16[1024,256]{1,0:T(8,128)(2,1)S(1)}, u32[]{:S(2)}, u32[]{:S(2)}) collective-permute-start(bf16[1024,256]{1,0:T(8,128)(2,1)S(1)} %copy-done), channel_id=1, source_target_pairs={{30,0},{31,1},{0,2},{1,3},{2,4},{3,5},{4,6},{5,7},{6,8},{7,9},{8,1... | collective-permute-start | bytes 1572872 | tf_op jit(solution)/shard_map/ppermute | solution.py:32
  935.1 26.5 %collective-permute-start.161 = (bf16[1024,256]{1,0:T(8,128)(2,1)S(1)}, bf16[1024,256]{1,0:T(8,128)(2,1)S(1)}, u32[]{:S(2)}, u32[]{:S(2)}) collective-permute-start(bf16[1024,256]{1,0:T(8,128)(2,1)S(1)} %copy-done), channel_id=1, source_target_pairs={{3,0},{4,1},{5,2},{6,3},{7,4},{8,5},{9,6},{10,7},{11,8},{12,9},{13... | collective-permute-start | bytes 1572872 | tf_op jit(solution)/shard_map/ppermute | solution.py:32
  949.9 27.8 %collective-permute-start.165 = (bf16[1024,256]{1,0:T(8,128)(2,1)S(1)}, bf16[1024,256]{1,0:T(8,128)(2,1)S(1)}, u32[]{:S(2)}, u32[]{:S(2)}) collective-permute-start(bf16[1024,256]{1,0:T(8,128)(2,1)S(1)} %copy-done), channel_id=1, source_target_pairs={{7,0},{8,1},{9,2},{10,3},{11,4},{12,5},{13,6},{14,7},{15,8},{16,9}... | collective-permute-start | bytes 1572872 | tf_op jit(solution)/shard_map/ppermute | solution.py:32
  1046.4 91.5 %collective-permute-start.166 = (bf16[1024,256]{1,0:T(8,128)(2,1)S(1)}, bf16[1024,256]{1,0:T(8,128)(2,1)S(1)}, u32[]{:S(2)}, u32[]{:S(2)}) collective-permute-start(bf16[1024,256]{1,0:T(8,128)(2,1)S(1)} %get-tuple-element.566), channel_id=1, source_target_pairs={{3,0},{4,1},{5,2},{6,3},{7,4},{8,5},{9,6},{10,7},{11,8},{12,9},{13... | collective-permute-start | bytes 1572872 | tf_op jit(solution)/shard_map/ppermute | solution.py:32
  1052.7 90.4 %collective-permute-start.171 = (bf16[1024,256]{1,0:T(8,128)(2,1)S(1)}, bf16[1024,256]{1,0:T(8,128)(2,1)S(1)}, u32[]{:S(2)}, u32[]{:S(2)}) collective-permute-start(bf16[1024,256]{1,0:T(8,128)(2,1)S(1)} %get-tuple-element.567), channel_id=1, source_target_pairs={{29,0},{30,1},{31,2},{0,3},{1,4},{2,5},{3,6},{4,7},{5,8},{6,9},{7,... | collective-permute-start | bytes 1572872 | tf_op jit(solution)/shard_map/ppermute | solution.py:32
  1064.6 95.6 %collective-permute-start.170 = (bf16[1024,256]{1,0:T(8,128)(2,1)S(1)}, bf16[1024,256]{1,0:T(8,128)(2,1)S(1)}, u32[]{:S(2)}, u32[]{:S(2)}) collective-permute-start(bf16[1024,256]{1,0:T(8,128)(2,1)S(1)} %get-tuple-element.568), channel_id=1, source_target_pairs={{30,0},{31,1},{0,2},{1,3},{2,4},{3,5},{4,6},{5,7},{6,8},{7,9},{8,1... | collective-permute-start | bytes 1572872 | tf_op jit(solution)/shard_map/ppermute | solution.py:32
  1137.4 39.7 %collective-permute-start.169 = (bf16[1024,256]{1,0:T(8,128)(2,1)S(1)}, bf16[1024,256]{1,0:T(8,128)(2,1)S(1)}, u32[]{:S(2)}, u32[]{:S(2)}) collective-permute-start(bf16[1024,256]{1,0:T(8,128)(2,1)S(1)} %get-tuple-element.569), channel_id=1, source_target_pairs={{31,0},{0,1},{1,2},{2,3},{3,4},{4,5},{5,6},{6,7},{7,8},{8,9},{9,10... | collective-permute-start | bytes 1572872 | tf_op jit(solution)/shard_map/ppermute | solution.py:32
  1137.4 39.7 %collective-permute-start.168 = (bf16[1024,256]{1,0:T(8,128)(2,1)S(1)}, bf16[1024,256]{1,0:T(8,128)(2,1)S(1)}, u32[]{:S(2)}, u32[]{:S(2)}) collective-permute-start(bf16[1024,256]{1,0:T(8,128)(2,1)S(1)} %get-tuple-element.570), channel_id=1, source_target_pairs={{1,0},{2,1},{3,2},{4,3},{5,4},{6,5},{7,6},{8,7},{9,8},{10,9},{11,1... | collective-permute-start | bytes 1572872 | tf_op jit(solution)/shard_map/ppermute | solution.py:32
  1137.9 39.2 %collective-permute-start.167 = (bf16[1024,256]{1,0:T(8,128)(2,1)S(1)}, bf16[1024,256]{1,0:T(8,128)(2,1)S(1)}, u32[]{:S(2)}, u32[]{:S(2)}) collective-permute-start(bf16[1024,256]{1,0:T(8,128)(2,1)S(1)} %get-tuple-element.571), channel_id=1, source_target_pairs={{2,0},{3,1},{4,2},{5,3},{6,4},{7,5},{8,6},{9,7},{10,8},{11,9},{12,... | collective-permute-start | bytes 1572872 | tf_op jit(solution)/shard_map/ppermute | solution.py:32
  (148 other events, 2141.8 us)
where the time goes:
time: 1190 us; the launch traced here: 1180 us
  starting transfers between devices  671 us (56%)
  waiting for transfers between devices  202 us (17%)
  loops' own time  116 us (10%)
  other arithmetic  77.8 us (7%)
  local copies, waits for them, and re-layouts  60 us (5%)
  matrix products  50.7 us (4%)
    ppermute x142, starting transfers between devices, passed_along_2(): return lax.ppermute(block, axis, route)  588 us
    ppermute x142, waiting for transfers between devices, passed_along_2(): return lax.ppermute(block, axis, route)  196 us
    ppermute x30, starting transfers between devices, passed_along(): lax.ppermute(value, axis, [(source, source + steps) for source in range(f...  83 us
    another operation x2, loops' own time, local(): lax.fori_loop(0, count, row_visit, initial_pair(2 * src_reach + 1))  47.1 us
    another operation x2, loops' own time, local(): lax.fori_loop(0, count, column_visit, initial_pair(2 * tgt_reach + 1))  44.8 us
    another operation x46, other arithmetic  34.1 us
    dot_general x5, matrix products, push_visit(): jnp.dot(weight, feat_window[tgt_pos], preferred_element_type=jnp.float32)  25.5 us
    dot_general x20, matrix products, cost_of(): lax.dot_general(src_window[src_pos], tgt_window[tgt_pos], (((0,), (0,)),...  25.3 us
  transfers between devices with their start and end apart: 172, of which 34 were waited for; matrix products, arithmetic and copies ran while one was open for 4% of the time, Pallas kernels for 0%

commit v1 on v0

v1 whole, which is shorter than its diff:
```python
import functools
import math

import jax
import jax.numpy as jnp
from jax import lax
from jax.experimental import pallas as pl
from jax.experimental.pallas import tpu as pltpu
from jax.sharding import PartitionSpec as P

REACH = 4
GROUP = 4
EPSILON = 0.1
LOWEST = -1e30
LOG2E = math.log2(math.e)
MESH = pl.DeviceIdType.MESH

PART = 64
DEPTH = 4 * PART
EXTRA = 3 * PART

WINDOW = 2 * REACH + 1
OFFSETS = [o for k in range(1, REACH + 1) for o in (k, -k)]
LIST_REACH = REACH + GROUP - 1
LIST_OFFSETS = [o for k in range(1, LIST_REACH + 1) for o in (k, -k)]


def split3(value):
    high = value.astype(jnp.bfloat16).astype(jnp.float32)
    rest = value - high
    middle = rest.astype(jnp.bfloat16).astype(jnp.float32)
    return high, middle, rest - middle


def extra_rows(first, second, cells):
    row = lax.broadcasted_iota(jnp.int32, (16, cells), 0)
    result = jnp.zeros((16, cells), jnp.float32)
    for at, part in enumerate(tuple(first) + tuple(second)):
        result = jnp.where(row == at, part, result)
    return result.astype(jnp.bfloat16)


def kernel(
    n, code_ref, x_ref, y_ref, feat_ref, smass_ref, tmass_ref,
    f_ref, g_ref, out_ref,
    lists, xw, yw, fw, xa, ya, ycol, padded, acc, aw, b1w, b2w,
    list_s, list_r, x_s, x_r, y_s, y_r, f_s, f_r, a_s, a_r, b1_s, b1_r, b2_s, b2_r, own_sem,
):
    dims, cells = x_ref.shape
    me = lax.axis_index("cells")
    scale = LOG2E / EPSILON
    factor = 2.0 * scale / dims

    def device(offset):
        return lax.rem(me + (offset + n), n)

    def copy(source, window, middle, offset, send, recv):
        return pltpu.make_async_remote_copy(
            src_ref=source,
            dst_ref=window.at[middle - offset],
            send_sem=send.at[middle - offset],
            recv_sem=recv.at[middle - offset],
            device_id=(device(offset),),
            device_id_type=MESH,
        )

    def send_all(source, window, send, recv, middle=REACH, offsets=OFFSETS):
        for offset in offsets:
            copy(source, window, middle, offset, send, recv).start()

    def arrived(source, window, send, recv, offset, middle=REACH):
        copy(source, window, middle, -offset, send, recv).wait_recv()

    def sent_all(source, window, send, recv, middle=REACH, offsets=OFFSETS):
        for offset in offsets:
            copy(source, window, middle, offset, send, recv).wait_send()

    barrier = pltpu.get_barrier_semaphore()
    for offset in LIST_OFFSETS:
        pl.semaphore_signal(barrier, inc=1, device_id=(device(offset),), device_id_type=MESH)

    padded[...] = jnp.zeros_like(padded)
    padded[0:dims, :] = x_ref[...].astype(jnp.float32)
    xw[REACH] = padded[...].astype(jnp.bfloat16)
    padded[0:dims, :] = y_ref[...].astype(jnp.float32)
    yw[REACH] = padded[...].astype(jnp.bfloat16)
    lists[LIST_REACH] = code_ref[...]

    pl.semaphore_wait(barrier, len(LIST_OFFSETS))
    send_all(lists.at[LIST_REACH], lists, list_s, list_r, LIST_REACH, LIST_OFFSETS)
    send_all(xw.at[REACH], xw, x_s, x_r)
    send_all(yw.at[REACH], yw, y_s, y_r)
    send_all(feat_ref, fw, f_s, f_r)
    own = pltpu.make_async_copy(feat_ref, fw.at[REACH], own_sem.at[0])
    own.start()

    one = jnp.ones((1, cells), jnp.float32)
    none = jnp.zeros((1, cells), jnp.float32)
    ones, nones = (one, one, one), (none, none, none)

    def squares(points):
        wide = points.astype(jnp.float32)
        return jnp.sum(wide * wide, axis=0, keepdims=True)

    def fill_source(w):
        wide = xw[w].astype(jnp.float32)
        for at, part in enumerate(split3(wide * factor)):
            xa[w, at * PART : (at + 1) * PART, :] = part.astype(jnp.bfloat16)
        xa[w, EXTRA:DEPTH, :] = jnp.zeros((PART, cells), jnp.bfloat16)

    def fill_target(ref, w):
        points = yw[w]
        for at in range(3):
            ref[at * PART : (at + 1) * PART, :] = points
        ref[EXTRA:DEPTH, :] = jnp.zeros((PART, cells), jnp.bfloat16)

    fill_source(REACH)
    fill_target(ya.at[REACH], REACH)
    fill_target(ycol, REACH)
    ycol[EXTRA : EXTRA + 16, :] = extra_rows(nones, ones, cells)

    for offset in LIST_OFFSETS:
        arrived(lists.at[LIST_REACH], lists, list_s, list_r, offset, LIST_REACH)
    codes = lists[...]

    def bias(source, target):
        hits = jnp.sum(jnp.where(codes == source * n + target, 1.0, 0.0), axis=0)
        return jnp.where(jnp.max(hits, axis=1, keepdims=True) > 0.5, 0.0, LOWEST)

    column_bias = [bias(device(w - REACH), me) for w in range(WINDOW)]
    row_bias = [bias(me, device(w - REACH)) for w in range(WINDOW)]

    for offset in OFFSETS:
        arrived(xw.at[REACH], xw, x_s, x_r, offset)
        fill_source(REACH + offset)
    for w in range(WINDOW):
        start = squares(xw[w]) * (-scale / dims) + column_bias[w]
        xa[w, EXTRA : EXTRA + 16, :] = extra_rows(ones, split3(start), cells)

    height = 256
    across = cells // height

    def reduced(lhs_ref, rhs_ref):
        def step(s, carry):
            highest, total = carry
            w, c = s // across, lax.rem(s, across)
            lhs = lhs_ref[w, :, pl.ds(pl.multiple_of(c * height, height), height)]
            scores = lax.dot_general(
                lhs, rhs_ref[...], (((0,), (0,)), ((), ())), preferred_element_type=jnp.float32
            ).reshape(height // 8, 8, cells)
            higher = jnp.maximum(highest, jnp.max(scores, axis=0))
            terms = jnp.sum(jnp.exp2(scores - higher[None]), axis=0)
            return higher, total * jnp.exp2(highest - higher) + terms

        highest, total = lax.fori_loop(
            0,
            WINDOW * across,
            step,
            (jnp.full((8, cells), LOWEST, jnp.float32), jnp.zeros((8, cells), jnp.float32)),
        )
        higher = jnp.max(highest, axis=0, keepdims=True)
        summed = jnp.sum(total * jnp.exp2(highest - higher), axis=0, keepdims=True)
        return higher + jnp.log(summed) * LOG2E

    b1w[REACH] = tmass_ref[...] * LOG2E - reduced(xa, ycol)
    send_all(b1w.at[REACH], b1w, b1_s, b1_r)
    for offset in OFFSETS:
        arrived(yw.at[REACH], yw, y_s, y_r, offset)
        fill_target(ya.at[REACH + offset], REACH + offset)
    for offset in [0] + OFFSETS:
        w = REACH + offset
        if offset != 0:
            arrived(b1w.at[REACH], b1w, b1_s, b1_r, offset)
        ya[w, EXTRA : EXTRA + 16, :] = extra_rows(split3(b1w[w] + row_bias[w]), nones, cells)

    aw[REACH] = smass_ref[...] * LOG2E - reduced(ya, xa.at[REACH])
    send_all(aw.at[REACH], aw, a_s, a_r)
    for offset in [0] + OFFSETS:
        w = REACH + offset
        if offset != 0:
            arrived(aw.at[REACH], aw, a_s, a_r, offset)
        xa[w, EXTRA : EXTRA + 16, :] = extra_rows(ones, split3(aw[w] + column_bias[w]), cells)

    b2w[REACH] = tmass_ref[...] * LOG2E - reduced(xa, ycol)
    send_all(b2w.at[REACH], b2w, b2_s, b2_r)
    g_ref[...] = b2w[REACH] * (1.0 / scale) + squares(yw[REACH]) * (1.0 / dims)
    for offset in [0] + OFFSETS:
        w = REACH + offset
        if offset != 0:
            arrived(b2w.at[REACH], b2w, b2_s, b2_r, offset)
        ya[w, EXTRA : EXTRA + 16, :] = extra_rows(split3(b2w[w] + row_bias[w]), nones, cells)

    own.wait()
    for offset in OFFSETS:
        arrived(feat_ref, fw, f_s, f_r, offset)
    acc[...] = jnp.zeros_like(acc)
    tall = 512
    pieces = cells // tall

    def mapping(s, carry):
        highest, total = carry
        w, c = s // pieces, lax.rem(s, pieces)
        start = pl.multiple_of(c * tall, tall)
        scores = lax.dot_general(
            ya[w, :, pl.ds(start, tall)], xa[REACH], (((0,), (0,)), ((), ())),
            preferred_element_type=jnp.float32,
        )
        higher = jnp.maximum(highest, jnp.max(scores, axis=0, keepdims=True))
        weight = jnp.exp2(scores - higher)
        shrink = jnp.exp2(highest - higher)
        terms = jnp.sum(weight.reshape(tall // 8, 8, cells), axis=0)
        acc[...] = acc[...] * shrink + lax.dot_general(
            fw[w, pl.ds(start, tall), :], weight.astype(jnp.bfloat16), (((0,), (0,)), ((), ())),
            preferred_element_type=jnp.float32,
        )
        return higher, total * shrink + terms

    highest, total = lax.fori_loop(
        0,
        WINDOW * pieces,
        mapping,
        (jnp.full((1, cells), LOWEST, jnp.float32), jnp.zeros((8, cells), jnp.float32)),
    )
    total = jnp.sum(total, axis=0, keepdims=True)
    last = smass_ref[...] * LOG2E - (highest + jnp.log(total) * LOG2E)
    f_ref[...] = last * (1.0 / scale) + squares(xw[REACH]) * (1.0 / dims)
    out_ref[...] = jnp.transpose(acc[...] * (1.0 / total)).astype(out_ref.dtype)

    sent_all(lists.at[LIST_REACH], lists, list_s, list_r, LIST_REACH, LIST_OFFSETS)
    sent_all(xw.at[REACH], xw, x_s, x_r)
    sent_all(yw.at[REACH], yw, y_s, y_r)
    sent_all(feat_ref, fw, f_s, f_r)
    sent_all(b1w.at[REACH], b1w, b1_s, b1_r)
    sent_all(aw.at[REACH], aw, a_s, a_r)
    sent_all(b2w.at[REACH], b2w, b2_s, b2_r)


def local(n, source_points, target_points, target_features, source_mass, target_mass, pair_list):
    cells = source_points.shape[1]
    width = target_features.shape[1]
    code = jnp.where(pair_list[2] == 1, pair_list[0] * n + pair_list[1], -1)
    code = jnp.pad(code[None, :], ((0, 0), (0, 128 - code.shape[0])), constant_values=-1)
    lists = 2 * LIST_REACH + 1
    vmem = pl.BlockSpec(memory_space=pltpu.VMEM)
    dma = pltpu.SemaphoreType.DMA
    potential, target, mapped = pl.pallas_call(
        functools.partial(kernel, n),
        out_shape=(
            jax.ShapeDtypeStruct((1, cells), jnp.float32),
            jax.ShapeDtypeStruct((1, cells), jnp.float32),
            jax.ShapeDtypeStruct((cells, width), jnp.bfloat16),
        ),
        in_specs=[vmem, vmem, vmem, pl.BlockSpec(memory_space=pl.ANY), vmem, vmem],
        out_specs=(vmem, vmem, vmem),
        scratch_shapes=[
            pltpu.VMEM((lists, 1, 128), jnp.int32),
            pltpu.VMEM((WINDOW, PART, cells), jnp.bfloat16),
            pltpu.VMEM((WINDOW, PART, cells), jnp.bfloat16),
            pltpu.VMEM((WINDOW, cells, width), jnp.bfloat16),
            pltpu.VMEM((WINDOW, DEPTH, cells), jnp.bfloat16),
            pltpu.VMEM((WINDOW, DEPTH, cells), jnp.bfloat16),
            pltpu.VMEM((DEPTH, cells), jnp.bfloat16),
            pltpu.VMEM((PART, cells), jnp.float32),
            pltpu.VMEM((width, cells), jnp.float32),
            pltpu.VMEM((WINDOW, 1, cells), jnp.float32),
            pltpu.VMEM((WINDOW, 1, cells), jnp.float32),
            pltpu.VMEM((WINDOW, 1, cells), jnp.float32),
            dma((lists,)), dma((lists,)),
        ]
        + [dma((WINDOW,))] * 12
        + [dma((1,))],
        compiler_params=pltpu.CompilerParams(
            collective_id=0, has_side_effects=True, vmem_limit_bytes=52 * 1024 * 1024
        ),
    )(
        code, source_points, target_points, target_features,
        source_mass.reshape(1, cells), target_mass.reshape(1, cells),
    )
    return potential.reshape(cells), target.reshape(cells), mapped


def solution(mesh):
    return jax.shard_map(
        functools.partial(local, mesh.shape["cells"]),
        mesh=mesh,
        in_specs=(
            P(None, "cells"),
            P(None, "cells"),
            P("cells", None),
            P("cells"),
            P("cells"),
            P(None, "cells"),
        ),
        out_specs=(P("cells"), P("cells"), P("cells", None)),
        check_vma=False,
    )
```

time: 1190 us -> 162 us (0.14)
  starting transfers between devices: 671 us -> 0 us
  waiting for transfers between devices: 202 us -> 0 us
  Pallas kernels: 0 us -> 155 us
  loops' own time: 116 us -> 0 us
  other arithmetic: 77.8 us -> 0.01 us
  local copies, waits for them, and re-layouts: 60 us -> 6.18 us
  matrix products: 50.7 us -> 0 us
    ppermute x172 -> x0, starting transfers between devices: 671 us -> none  [the longest x142 588 us: passed_along_2(): return lax.ppermute(block, axis, route)]
    ppermute x172 -> x0, waiting for transfers between devices: 202 us -> none  [the longest x142 196 us: passed_along_2(): return lax.ppermute(block, axis, route)]
    pallas_call x0 -> x1, Pallas kernels: none -> 155 us  [local(): pl.pallas_call(functools.partial(kernel, n), out_shape=(jax.ShapeDtypeStr...]
    another operation x5 -> x0, loops' own time: 116 us -> none  [the longest x2 47.1 us: local(): lax.fori_loop(0, count, row_visit, initial_pair(2 * src_reach + 1))]
    dot_general x25 -> x0, matrix products: 50.7 us -> none  [the longest x5 25.5 us: push_visit(): jnp.dot(weight, feat_window[tgt_pos], preferred_element_type=jnp.float32)]
    reduce_sum x23 -> x0, other arithmetic: 40.3 us -> none  [the longest x10 19.2 us: row_visit(): summed = jnp.sum(jnp.exp(scores - higher[:, None]), axis=1)]
    another operation x52 -> x0, other arithmetic: 34.1 us -> none
    dynamic_slice x105 -> x0, local copies, waits for them, and re-layouts: 31.2 us -> none  [the longest x10 6.17 us: row_visit(): src_pos = src_slots[slot_index]]
  transfers between devices with their start and end apart: 172 -> 0, of which waited for: 34 -> 0; matrix products, arithmetic and copies ran while one was open for 4% -> 0% of each run, Pallas kernels for 0% -> 0%
where the time goes in v1:
time: 162 us
  Pallas kernels  155 us (96%)
  local copies, waits for them, and re-layouts  6.18 us (4%)
    pallas_call x1, Pallas kernels, local(): pl.pallas_call(functools.partial(kernel, n), out_shape=(jax.ShapeDtypeStr...  155 us
    unnamed x15, local copies, waits for them, and re-layouts  6.17 us

profile of v1, /device:TPU:1, one launch (start us, length us, event | category | flops | bytes accessed | tf_op | source)
XLA Modules:
  0.0 161.7 jit_solution(15799823503054397867)
XLA Ops:
  0.6 0.0 copy-start.5
  0.6 0.0 copy-start.3
  0.7 0.7 copy-done.5
  1.3 0.0 copy-done.3
  1.3 0.0 copy-start
  1.3 1.0 copy-done
  2.4 0.0 copy-start.1
  2.4 0.9 copy-done.1
  3.3 0.0 copy-start.2
  3.3 0.9 copy-done.2
  4.2 0.0 copy-start.4
  4.2 0.7 copy-done.4
  4.9 154.9 %shard_map.85 = (f32[1,1024]{1,0:T(1,128)S(1)}, f32[1,1024]{1,0:T(1,128)S(1)}, bf16[1024,256]{1,0:T(8,128)(2,1)S(1)}) custom-call(s32[1,128]{1,0:T(1,128)S(1)} %pad.4.code_ref, bf16[50,1024]{1,0:T(8,128)(2,1)S(1)} %copy-done.1, bf16[50,1024]{1,0:T(8,128)(2,1)S(1)} %copy-done.2, bf16[1024,256]{1,0:T(8,128)(2,1)S(1)} %copy-done, f32[1,1024]{1,0:T(1,128)S(1)} %bitcast.4, ...), custom_call_target="tpu_custom_call" | custom-call | tf_op jit(solution)/shard_map/pallas_call | solution.py:246
  159.7 0.6 copy.12
  160.3 0.6 copy.13
  160.9 0.8 copy.14
  (2 shorter events, 0.0 us)
Async XLA Ops:
  0.6 0.7 copy-start.5
  0.6 0.7 copy-start.3
  1.3 1.0 copy-start
  2.4 0.9 copy-start.1
  3.3 0.9 copy-start.2
  4.2 0.7 copy-start.4

commit v2 on v1

--- a/solution.py
+++ b/solution.py
@@ -21,6 +21,8 @@
 
 WINDOW = 2 * REACH + 1
 OFFSETS = [o for k in range(1, REACH + 1) for o in (k, -k)]
+EVEN = [o for o in OFFSETS if o % 2 == 0]
+RELAYED = [w for w in range(WINDOW) if (w - REACH) % 2 != 0]
 LIST_REACH = REACH + GROUP - 1
 LIST_OFFSETS = [o for k in range(1, LIST_REACH + 1) for o in (k, -k)]
 
@@ -75,6 +77,33 @@
         for offset in offsets:
             copy(source, window, middle, offset, send, recv).wait_send()
 
+    core = lax.rem(me, 2)
+    sibling = me + 1 - 2 * core
+
+    def relay(window, w, send, recv):
+        return pltpu.make_async_remote_copy(
+            src_ref=window.at[w + 1 - 2 * core],
+            dst_ref=window.at[w],
+            send_sem=send.at[w],
+            recv_sem=recv.at[w],
+            device_id=(sibling,),
+            device_id_type=MESH,
+        )
+
+    def forward(source, window, send, recv):
+        for offset in EVEN:
+            arrived(source, window, send, recv, offset)
+        for w in RELAYED:
+            relay(window, w, send, recv).start()
+
+    def relays_arrived(window, send, recv):
+        for w in RELAYED:
+            relay(window, w, send, recv).wait_recv()
+
+    def relays_sent(window, send, recv):
+        for w in RELAYED:
+            relay(window, w, send, recv).wait_send()
+
     barrier = pltpu.get_barrier_semaphore()
     for offset in LIST_OFFSETS:
         pl.semaphore_signal(barrier, inc=1, device_id=(device(offset),), device_id_type=MESH)
@@ -88,9 +117,8 @@
 
     pl.semaphore_wait(barrier, len(LIST_OFFSETS))
     send_all(lists.at[LIST_REACH], lists, list_s, list_r, LIST_REACH, LIST_OFFSETS)
-    send_all(xw.at[REACH], xw, x_s, x_r)
-    send_all(yw.at[REACH], yw, y_s, y_r)
-    send_all(feat_ref, fw, f_s, f_r)
+    send_all(xw.at[REACH], xw, x_s, x_r, offsets=EVEN)
+    send_all(yw.at[REACH], yw, y_s, y_r, offsets=EVEN)
     own = pltpu.make_async_copy(feat_ref, fw.at[REACH], own_sem.at[0])
     own.start()
 
@@ -130,9 +158,12 @@
     column_bias = [bias(device(w - REACH), me) for w in range(WINDOW)]
     row_bias = [bias(me, device(w - REACH)) for w in range(WINDOW)]
 
-    for offset in OFFSETS:
-        arrived(xw.at[REACH], xw, x_s, x_r, offset)
+    forward(xw.at[REACH], xw, x_s, x_r)
+    for offset in EVEN:
         fill_source(REACH + offset)
+    relays_arrived(xw, x_s, x_r)
+    for w in RELAYED:
+        fill_source(w)
     for w in range(WINDOW):
         start = squares(xw[w]) * (-scale / dims) + column_bias[w]
         xa[w, EXTRA : EXTRA + 16, :] = extra_rows(ones, split3(start), cells)
@@ -157,6 +188,7 @@
             WINDOW * across,
             step,
             (jnp.full((8, cells), LOWEST, jnp.float32), jnp.zeros((8, cells), jnp.float32)),
+            unroll=2,
         )
         higher = jnp.max(highest, axis=0, keepdims=True)
         summed = jnp.sum(total * jnp.exp2(highest - higher), axis=0, keepdims=True)
@@ -164,15 +196,19 @@
 
     b1w[REACH] = tmass_ref[...] * LOG2E - reduced(xa, ycol)
     send_all(b1w.at[REACH], b1w, b1_s, b1_r)
-    for offset in OFFSETS:
-        arrived(yw.at[REACH], yw, y_s, y_r, offset)
+    forward(yw.at[REACH], yw, y_s, y_r)
+    for offset in EVEN:
         fill_target(ya.at[REACH + offset], REACH + offset)
+    relays_arrived(yw, y_s, y_r)
+    for w in RELAYED:
+        fill_target(ya.at[w], w)
     for offset in [0] + OFFSETS:
         w = REACH + offset
         if offset != 0:
             arrived(b1w.at[REACH], b1w, b1_s, b1_r, offset)
         ya[w, EXTRA : EXTRA + 16, :] = extra_rows(split3(b1w[w] + row_bias[w]), nones, cells)
 
+    send_all(feat_ref, fw, f_s, f_r, offsets=EVEN)
     aw[REACH] = smass_ref[...] * LOG2E - reduced(ya, xa.at[REACH])
     send_all(aw.at[REACH], aw, a_s, a_r)
     for offset in [0] + OFFSETS:
@@ -183,6 +219,8 @@
 
     b2w[REACH] = tmass_ref[...] * LOG2E - reduced(xa, ycol)
     send_all(b2w.at[REACH], b2w, b2_s, b2_r)
+    own.wait()
+    forward(feat_ref, fw, f_s, f_r)
     g_ref[...] = b2w[REACH] * (1.0 / scale) + squares(yw[REACH]) * (1.0 / dims)
     for offset in [0] + OFFSETS:
         w = REACH + offset
@@ -190,9 +228,7 @@
             arrived(b2w.at[REACH], b2w, b2_s, b2_r, offset)
         ya[w, EXTRA : EXTRA + 16, :] = extra_rows(split3(b2w[w] + row_bias[w]), nones, cells)
 
-    own.wait()
-    for offset in OFFSETS:
-        arrived(feat_ref, fw, f_s, f_r, offset)
+    relays_arrived(fw, f_s, f_r)
     acc[...] = jnp.zeros_like(acc)
     tall = 512
     pieces = cells // tall
@@ -227,9 +263,12 @@
     out_ref[...] = jnp.transpose(acc[...] * (1.0 / total)).astype(out_ref.dtype)
 
     sent_all(lists.at[LIST_REACH], lists, list_s, list_r, LIST_REACH, LIST_OFFSETS)
-    sent_all(xw.at[REACH], xw, x_s, x_r)
-    sent_all(yw.at[REACH], yw, y_s, y_r)
-    sent_all(feat_ref, fw, f_s, f_r)
+    sent_all(xw.at[REACH], xw, x_s, x_r, offsets=EVEN)
+    sent_all(yw.at[REACH], yw, y_s, y_r, offsets=EVEN)
+    sent_all(feat_ref, fw, f_s, f_r, offsets=EVEN)
+    relays_sent(xw, x_s, x_r)
+    relays_sent(yw, y_s, y_r)
+    relays_sent(fw, f_s, f_r)
     sent_all(b1w.at[REACH], b1w, b1_s, b1_r)
     sent_all(aw.at[REACH], aw, a_s, a_r)
     sent_all(b2w.at[REACH], b2w, b2_s, b2_r)

time: 162 us -> 120 us (0.74)
  Pallas kernels: 155 us -> 113 us
    pallas_call x1, Pallas kernels: 155 us -> 113 us  [local(): pl.pallas_call(functools.partial(kernel, n), out_shape=(jax.ShapeDtypeStr...]
where the time goes in v2:
time: 120 us
  Pallas kernels  113 us (94%)
  local copies, waits for them, and re-layouts  6.18 us (5%)
    pallas_call x1, Pallas kernels, local(): pl.pallas_call(functools.partial(kernel, n), out_shape=(jax.ShapeDtypeStr...  113 us
    unnamed x15, local copies, waits for them, and re-layouts  6.17 us

profile of v2, /device:TPU:1, one launch (start us, length us, event | category | flops | bytes accessed | tf_op | source)
XLA Modules:
  0.0 119.5 jit_solution(7275678064088967275)
XLA Ops:
  0.6 0.0 copy-start.5
  0.6 0.0 copy-start.3
  0.7 0.7 copy-done.5
  1.3 0.0 copy-done.3
  1.3 0.0 copy-start
  1.3 1.0 copy-done
  2.4 0.0 copy-start.1
  2.4 0.9 copy-done.1
  3.3 0.0 copy-start.2
  3.3 0.9 copy-done.2
  4.2 0.0 copy-start.4
  4.2 0.7 copy-done.4
  4.9 112.7 %shard_map.85 = (f32[1,1024]{1,0:T(1,128)S(1)}, f32[1,1024]{1,0:T(1,128)S(1)}, bf16[1024,256]{1,0:T(8,128)(2,1)S(1)}) custom-call(s32[1,128]{1,0:T(1,128)S(1)} %pad.4.code_ref, bf16[50,1024]{1,0:T(8,128)(2,1)S(1)} %copy-done.1, bf16[50,1024]{1,0:T(8,128)(2,1)S(1)} %copy-done.2, bf16[1024,256]{1,0:T(8,128)(2,1)S(1)} %copy-done, f32[1,1024]{1,0:T(1,128)S(1)} %bitcast.4, ...), custom_call_target="tpu_custom_call" | custom-call | tf_op jit(solution)/shard_map/pallas_call | solution.py:285
  117.5 0.6 copy.12
  118.1 0.6 copy.13
  118.7 0.8 copy.14
  (2 shorter events, 0.0 us)
Async XLA Ops:
  0.6 0.7 copy-start.5
  0.6 0.7 copy-start.3
  1.3 1.0 copy-start
  2.4 0.9 copy-start.1
  3.3 0.9 copy-start.2
  4.2 0.7 copy-start.4

commit v3 on v2

--- a/solution.py
+++ b/solution.py
@@ -10,6 +10,7 @@
 
 REACH = 4
 GROUP = 4
+NEIGH = 7
 EPSILON = 0.1
 LOWEST = -1e30
 LOG2E = math.log2(math.e)
@@ -45,7 +46,7 @@
 def kernel(
     n, code_ref, x_ref, y_ref, feat_ref, smass_ref, tmass_ref,
     f_ref, g_ref, out_ref,
-    lists, xw, yw, fw, xa, ya, ycol, padded, acc, aw, b1w, b2w,
+    paired, lists, xw, yw, fw, xa, ya, ycol, padded, acc, aw, b1w, b2w,
     list_s, list_r, x_s, x_r, y_s, y_r, f_s, f_r, a_s, a_r, b1_s, b1_r, b2_s, b2_r, own_sem,
 ):
     dims, cells = x_ref.shape
@@ -156,7 +157,17 @@
         return jnp.where(jnp.max(hits, axis=1, keepdims=True) > 0.5, 0.0, LOWEST)
 
     column_bias = [bias(device(w - REACH), me) for w in range(WINDOW)]
-    row_bias = [bias(me, device(w - REACH)) for w in range(WINDOW)]
+    live = [
+        jnp.max(jnp.where(codes == me * n + device(w - REACH), 1, 0)) for w in range(WINDOW)
+    ]
+    entries = [jnp.int32(REACH)] * NEIGH
+    rank = jnp.int32(0)
+    for w in range(WINDOW):
+        for k in range(NEIGH):
+            entries[k] = jnp.where((rank == k) & (live[w] == 1), w, entries[k])
+        rank = rank + live[w]
+    for k in range(NEIGH):
+        paired[k] = entries[k]
 
     forward(xw.at[REACH], xw, x_s, x_r)
     for offset in EVEN:
@@ -171,10 +182,10 @@
     height = 256
     across = cells // height
 
-    def reduced(lhs_ref, rhs_ref):
+    def reduced(lhs_ref, rhs_ref, visits, entry):
         def step(s, carry):
             highest, total = carry
-            w, c = s // across, lax.rem(s, across)
+            w, c = entry(s // across), lax.rem(s, across)
             lhs = lhs_ref[w, :, pl.ds(pl.multiple_of(c * height, height), height)]
             scores = lax.dot_general(
                 lhs, rhs_ref[...], (((0,), (0,)), ((), ())), preferred_element_type=jnp.float32
@@ -185,7 +196,7 @@
 
         highest, total = lax.fori_loop(
             0,
-            WINDOW * across,
+            visits * across,
             step,
             (jnp.full((8, cells), LOWEST, jnp.float32), jnp.zeros((8, cells), jnp.float32)),
             unroll=2,
@@ -194,7 +205,7 @@
         summed = jnp.sum(total * jnp.exp2(highest - higher), axis=0, keepdims=True)
         return higher + jnp.log(summed) * LOG2E
 
-    b1w[REACH] = tmass_ref[...] * LOG2E - reduced(xa, ycol)
+    b1w[REACH] = tmass_ref[...] * LOG2E - reduced(xa, ycol, WINDOW, lambda w: w)
     send_all(b1w.at[REACH], b1w, b1_s, b1_r)
     forward(yw.at[REACH], yw, y_s, y_r)
     for offset in EVEN:
@@ -206,10 +217,10 @@
         w = REACH + offset
         if offset != 0:
             arrived(b1w.at[REACH], b1w, b1_s, b1_r, offset)
-        ya[w, EXTRA : EXTRA + 16, :] = extra_rows(split3(b1w[w] + row_bias[w]), nones, cells)
+        ya[w, EXTRA : EXTRA + 16, :] = extra_rows(split3(b1w[w]), nones, cells)
 
     send_all(feat_ref, fw, f_s, f_r, offsets=EVEN)
-    aw[REACH] = smass_ref[...] * LOG2E - reduced(ya, xa.at[REACH])
+    aw[REACH] = smass_ref[...] * LOG2E - reduced(ya, xa.at[REACH], NEIGH, lambda k: paired[k])
     send_all(aw.at[REACH], aw, a_s, a_r)
     for offset in [0] + OFFSETS:
         w = REACH + offset
@@ -217,7 +228,7 @@
             arrived(aw.at[REACH], aw, a_s, a_r, offset)
         xa[w, EXTRA : EXTRA + 16, :] = extra_rows(ones, split3(aw[w] + column_bias[w]), cells)
 
-    b2w[REACH] = tmass_ref[...] * LOG2E - reduced(xa, ycol)
+    b2w[REACH] = tmass_ref[...] * LOG2E - reduced(xa, ycol, WINDOW, lambda w: w)
     send_all(b2w.at[REACH], b2w, b2_s, b2_r)
     own.wait()
     forward(feat_ref, fw, f_s, f_r)
@@ -226,7 +237,7 @@
         w = REACH + offset
         if offset != 0:
             arrived(b2w.at[REACH], b2w, b2_s, b2_r, offset)
-        ya[w, EXTRA : EXTRA + 16, :] = extra_rows(split3(b2w[w] + row_bias[w]), nones, cells)
+        ya[w, EXTRA : EXTRA + 16, :] = extra_rows(split3(b2w[w]), nones, cells)
 
     relays_arrived(fw, f_s, f_r)
     acc[...] = jnp.zeros_like(acc)
@@ -235,7 +246,7 @@
 
     def mapping(s, carry):
         highest, total = carry
-        w, c = s // pieces, lax.rem(s, pieces)
+        w, c = paired[s // pieces], lax.rem(s, pieces)
         start = pl.multiple_of(c * tall, tall)
         scores = lax.dot_general(
             ya[w, :, pl.ds(start, tall)], xa[REACH], (((0,), (0,)), ((), ())),
@@ -253,7 +264,7 @@
 
     highest, total = lax.fori_loop(
         0,
-        WINDOW * pieces,
+        NEIGH * pieces,
         mapping,
         (jnp.full((1, cells), LOWEST, jnp.float32), jnp.zeros((8, cells), jnp.float32)),
     )
@@ -292,6 +303,7 @@
         in_specs=[vmem, vmem, vmem, pl.BlockSpec(memory_space=pl.ANY), vmem, vmem],
         out_specs=(vmem, vmem, vmem),
         scratch_shapes=[
+            pltpu.SMEM((NEIGH,), jnp.int32),
             pltpu.VMEM((lists, 1, 128), jnp.int32),
             pltpu.VMEM((WINDOW, PART, cells), jnp.bfloat16),
             pltpu.VMEM((WINDOW, PART, cells), jnp.bfloat16),

time: 120 us -> 116 us (0.967)
  Pallas kernels: 113 us -> 108 us
    pallas_call x1, Pallas kernels: 113 us -> 108 us  [local(): pl.pallas_call(functools.partial(kernel, n), out_shape=(jax.ShapeDtypeStr...]
where the time goes in v3:
time: 116 us; the launch traced here: 115 us
  Pallas kernels  108 us (93%)
  local copies, waits for them, and re-layouts  6.18 us (5%)
    pallas_call x1, Pallas kernels, local(): pl.pallas_call(functools.partial(kernel, n), out_shape=(jax.ShapeDtypeStr...  108 us
    unnamed x15, local copies, waits for them, and re-layouts  6.17 us

profile of v3, /device:TPU:1, one launch (start us, length us, event | category | flops | bytes accessed | tf_op | source)
XLA Modules:
  0.0 115.2 jit_solution(13104032129283650174)
XLA Ops:
  0.6 0.0 copy-start.5
  0.6 0.0 copy-start.3
  0.7 0.7 copy-done.5
  1.3 0.0 copy-done.3
  1.3 0.0 copy-start
  1.3 1.0 copy-done
  2.4 0.0 copy-start.1
  2.4 0.9 copy-done.1
  3.3 0.0 copy-start.2
  3.3 0.9 copy-done.2
  4.2 0.0 copy-start.4
  4.2 0.7 copy-done.4
  4.9 108.4 %shard_map.85 = (f32[1,1024]{1,0:T(1,128)S(1)}, f32[1,1024]{1,0:T(1,128)S(1)}, bf16[1024,256]{1,0:T(8,128)(2,1)S(1)}) custom-call(s32[1,128]{1,0:T(1,128)S(1)} %pad.4.code_ref, bf16[50,1024]{1,0:T(8,128)(2,1)S(1)} %copy-done.1, bf16[50,1024]{1,0:T(8,128)(2,1)S(1)} %copy-done.2, bf16[1024,256]{1,0:T(8,128)(2,1)S(1)} %copy-done, f32[1,1024]{1,0:T(1,128)S(1)} %bitcast.4, ...), custom_call_target="tpu_custom_call" | custom-call | tf_op jit(solution)/shard_map/pallas_call | solution.py:296
  113.2 0.6 copy.12
  113.8 0.6 copy.13
  114.4 0.8 copy.14
  (2 shorter events, 0.0 us)
Async XLA Ops:
  0.6 0.7 copy-start.5
  0.6 0.7 copy-start.3
  1.3 1.0 copy-start
  2.4 0.9 copy-start.1
  3.3 0.9 copy-start.2
  4.2 0.7 copy-start.4
